TPU v7x, 32 devices: a whole 2x2x4 slice. The times are simulated.
32 devices in a mesh: grp: 2 (over y), ew: 4 (over z), ns: 2 (over x), lvl: 2 (over core).
Axes of the slice: x: 2, y: 2, z: 4, core: 2. Of those that a mesh axis runs over, the one named last changes fastest.
Arguments:
- probe_fine: int32 [8, 128, 512], P('lvl', 'ew', 'ns'), may hold values from 0 to 1
- probe_coarse: int32 [8, 64, 256], P('lvl', 'ew', 'ns'), may hold values from 0 to 1
- kappa_fine: float32 [256, 512], P(('grp', 'ew'), 'ns'), parts along dimension 0, may hold values from 0.2 to 2
- kappa_coarse: float32 [128, 256], P(('grp', 'ew'), 'ns'), parts along dimension 0, may hold values from 0.2 to 2
- phi_tiles: float32 [1024, 128, 128], P(('ew', 'ns')), may hold values from -0.5 to 0.5
- obs_weight: float32 [2048, 128], P(('grp', 'ew', 'ns')), parts along dimension 0, may hold values from 4 to 40
- block_index: int32 [1024], P(('ew', 'ns')), may hold values from 0 to 85, as said below
- block_count: int32 [8], P(('ew', 'ns')), may hold values from 2 to 128, as said below
Outputs:
- solve_fine: float32 [16, 128, 512], P(('grp', 'lvl'), 'ew', 'ns'), parts along dimension 0
- solve_coarse: float32 [16, 64, 256], P(('grp', 'lvl'), 'ew', 'ns'), parts along dimension 0
- resid_fine: float32 [16, 128, 512], P(('grp', 'lvl'), 'ew', 'ns'), parts along dimension 0
- resid_coarse: float32 [16, 64, 256], P(('grp', 'lvl'), 'ew', 'ns'), parts along dimension 0
There are 2 independent parts, one for each index of `grp`. A program takes and returns all parts, laid end to end along the dimension named above; an argument that names none is the same for every part. Nothing has to cross between parts.
Inputs may be any that keep to these rules, and one draw needn't show every extreme that they name: `block_count`: every device has 2 or more live blocks, and only blocks below its count carry observations; some device has all 128 slots live. `block_index`: A block's tile is one of its own device's 86 tiles, in the order of the tile list; each device's first block names a tile of its western outside row (fine or coarse) and its second block a tile of its eastern outside row.
All inputs are finite; a program needn't handle non-finite values.
Results may differ from a plain program's by a relative error of at most 0.0003.
Values sent between devices are 32-bit elements; how exact they have to be, the bound alone decides.
A program may use at most 64 MiB of HBM per device.

v0:
```python
import jax
import jax.numpy as jnp
from jax import lax
from jax.sharding import PartitionSpec as P

ITERS = 2


def with_halo(block, sides, width):
    for axis, dim in sides:
        count = lax.axis_size(axis)
        forward = [(i, i + 1) for i in range(count - 1)]
        backward = [(target, source) for source, target in forward]
        low = lax.ppermute(
            lax.slice_in_dim(block, block.shape[dim] - width, None, axis=dim), axis, forward
        )
        high = lax.ppermute(lax.slice_in_dim(block, 0, width, axis=dim), axis, backward)
        block = jnp.concatenate([low, block, high], axis=dim)
    return block


def shifted(block, axis, distance):
    devices = range(lax.axis_size(axis))
    route = [(i - distance, i) for i in devices if i - distance in devices]
    return lax.ppermute(block, axis, route)


def apply_sar(padded, kappa):
    centre = padded[:, 1:-1, 1:-1]
    beside_all = (
        padded[:, 2:, 1:-1] + padded[:, :-2, 1:-1] + padded[:, 1:-1, 2:] + padded[:, 1:-1, :-2]
    )
    return (4.0 + kappa) * centre - beside_all


def fine_faces(field):
    return with_halo(field, (("ew", 1), ("ns", 2)), 1)


def coarse_faces(field):
    return with_halo(field, (("ew", 1), ("ns", 2)), 1)


def local_products(first_fine, first_coarse, second_fine, second_coarse):
    return jnp.sum(first_fine * second_fine, axis=(1, 2)) + jnp.sum(
        first_coarse * second_coarse, axis=(1, 2)
    )


def local(
    probe_fine,
    probe_coarse,
    kappa_fine,
    kappa_coarse,
    phi_tiles,
    obs_weight,
    block_index,
    block_count,
):
    probes, rows, width = probe_fine.shape
    half_rows = probe_coarse.shape[1]
    tile = phi_tiles.shape[1]
    blocks = phi_tiles.shape[0]
    fine_count = (rows + 2) * (width // tile)
    tile_total = fine_count + half_rows + 2
    live = (jnp.arange(blocks, dtype=jnp.int32) < block_count[0]).astype(jnp.float32)
    weights = (obs_weight * live[:, None])[None]
    onehot = (block_index[:, None] == jnp.arange(tile_total, dtype=jnp.int32)[None, :]).astype(
        jnp.float32
    )
    resid_fine = (2 * probe_fine - 1).astype(jnp.float32)
    resid_coarse = (2 * probe_coarse - 1).astype(jnp.float32)
    solve_fine = jnp.zeros_like(resid_fine)
    solve_coarse = jnp.zeros_like(resid_coarse)

    def squares(first_fine, first_coarse):
        return lax.psum(
            local_products(first_fine, first_coarse, first_fine, first_coarse), ("ew", "ns")
        )

    direction_fine, direction_coarse = (resid_fine, resid_coarse)
    norm_now = squares(resid_fine, resid_coarse)
    for iteration in range(ITERS):
        halo_fine = fine_faces(direction_fine)
        halo_coarse = coarse_faces(direction_coarse)
        prior_fine = apply_sar(fine_faces(apply_sar(halo_fine, kappa_fine)), kappa_fine)
        prior_coarse = apply_sar(coarse_faces(apply_sar(halo_coarse, kappa_coarse)), kappa_coarse)
        rows_fine = halo_fine[:, :, 1:-1]
        rows_coarse = halo_coarse[:, :, 1:-1]
        ext = jnp.concatenate([rows_fine.reshape(probes, fine_count, tile), rows_coarse], axis=1)
        picked = jnp.take(ext, block_index, axis=1)
        seen = jnp.einsum(
            "bij,pbj->pbi",
            phi_tiles,
            picked,
            precision=lax.Precision.HIGHEST,
            preferred_element_type=jnp.float32,
        )
        scaled = seen * weights
        back = jnp.einsum(
            "bij,pbi->pbj",
            phi_tiles,
            scaled,
            precision=lax.Precision.HIGHEST,
            preferred_element_type=jnp.float32,
        )
        adjoint = jnp.einsum("pbj,bt->ptj", back, onehot, precision=lax.Precision.HIGHEST)
        adj_fine = adjoint[:, :fine_count].reshape(probes, rows + 2, width)
        adj_coarse = adjoint[:, fine_count:]
        west_row = jnp.concatenate([adj_fine[:, 0], adj_coarse[:, 0]], axis=-1)
        east_row = jnp.concatenate([adj_fine[:, -1], adj_coarse[:, -1]], axis=-1)
        from_next = shifted(west_row, "ew", -1)
        from_prev = shifted(east_row, "ew", 1)
        inner_fine = adj_fine[:, 1:-1]
        inner_fine = (
            inner_fine.at[:, 0].add(from_prev[:, :width]).at[:, -1].add(from_next[:, :width])
        )
        inner_coarse = adj_coarse[:, 1:-1]
        inner_coarse = (
            inner_coarse.at[:, 0].add(from_prev[:, width:]).at[:, -1].add(from_next[:, width:])
        )
        image_fine = prior_fine + inner_fine
        image_coarse = prior_coarse + inner_coarse
        curve = lax.psum(
            local_products(direction_fine, direction_coarse, image_fine, image_coarse), ("ew", "ns")
        )
        alpha = (norm_now / curve)[:, None, None]
        solve_fine = solve_fine + alpha * direction_fine
        solve_coarse = solve_coarse + alpha * direction_coarse
        resid_fine = resid_fine - alpha * image_fine
        resid_coarse = resid_coarse - alpha * image_coarse
        if iteration + 1 < ITERS:
            norm_next = squares(resid_fine, resid_coarse)
            ratio = (norm_next / norm_now)[:, None, None]
            direction_fine = resid_fine + ratio * direction_fine
            direction_coarse = resid_coarse + ratio * direction_coarse
            norm_now = norm_next
    return (solve_fine, solve_coarse, resid_fine, resid_coarse)


def solution(mesh):
    in_specs = (
        P("lvl", "ew", "ns"),
        P("lvl", "ew", "ns"),
        P(("grp", "ew"), "ns"),
        P(("grp", "ew"), "ns"),
        P(("ew", "ns"), None, None),
        P(("grp", "ew", "ns"), None),
        P(("ew", "ns")),
        P(("ew", "ns")),
    )
    out_specs = (
        P(("grp", "lvl"), "ew", "ns"),
        P(("grp", "lvl"), "ew", "ns"),
        P(("grp", "lvl"), "ew", "ns"),
        P(("grp", "lvl"), "ew", "ns"),
    )
    return jax.shard_map(local, mesh=mesh, in_specs=in_specs, out_specs=out_specs, check_vma=False)
```

profile of v0, /device:TPU:0, one launch (start us, length us, event | category | flops | bytes accessed | tf_op | source)
XLA Modules:
  0.0 239.9 jit_solution(14725809653699780462)
XLA Ops:
  1.4 1.3 collective-permute-start.9
  2.7 5.6 %collective-permute-start.8 = (f32[4,1,128]{2,1,0:T(1,128)S(1)}, f32[4,1,128]{2,1,0:T(1,128)S(1)}, u32[]{:S(2)}, u32[]{:S(2)}) collective-permute-start(f32[4,1,128]{2,1,0:T(1,128)S(1)} %get-tuple-element.164), channel_id=1, source_target_pairs={{0,4},{4,8},{8,12},{1,5},{5,9},{9,13},{2,6},{6,10},{10,14},{3,7},{... | collective-permute-start | bytes 6152 | tf_op jit(solution)/shard_map/ppermute | solution.py:14
  9.3 1.3 collective-permute-start
  10.6 4.6 %collective-permute-start.1 = (f32[4,1,256]{2,0,1:T(4,128)S(1)}, f32[4,1,256]{2,0,1:T(4,128)S(1)}, u32[]{:S(2)}, u32[]{:S(2)}) collective-permute-start(f32[4,1,256]{2,0,1:T(4,128)S(1)} %get-tuple-element.146), channel_id=1, source_target_pairs={{0,4},{4,8},{8,12},{1,5},{5,9},{9,13},{2,6},{6,10},{10,14},{3,7},{... | collective-permute-start | bytes 12296 | tf_op jit(solution)/shard_map/ppermute | solution.py:14
  19.6 3.8 %collective-permute-start.13 = (f32[4,18,1]{2,1,0:T(8,128)S(1)}, f32[4,18,1]{2,1,0:T(8,128)S(1)}, u32[]{:S(2)}, u32[]{:S(2)}) collective-permute-start(f32[4,18,1]{2,1,0:T(8,128)S(1)} %get-tuple-element.155), channel_id=1, source_target_pairs={{0,2},{1,3},{4,6},{5,7},{8,10},{9,11},{12,14},{13,15},{16,18},{17,... | collective-permute-start | bytes 872 | tf_op jit(solution)/shard_map/ppermute | solution.py:14
  23.5 1.3 collective-permute-start.12
  25.2 4.3 %collective-permute-done.12 = f32[4,18,1]{2,1,0:T(8,128)S(1)} collective-permute-done((f32[4,18,1]{2,1,0:T(8,128)S(1)}, f32[4,18,1]{2,1,0:T(8,128)S(1)}, u32[]{:S(2)}, u32[]{:S(2)}) %collective-permute-start.12) | collective-permute-done | bytes 320 | tf_op jit(solution)/shard_map/ppermute | solution.py:17
  29.6 1.3 collective-permute-start.14
  30.9 4.5 %collective-permute-start.15 = (f32[4,1,128]{2,1,0:T(1,128)S(1)}, f32[4,1,128]{2,1,0:T(1,128)S(1)}, u32[]{:S(2)}, u32[]{:S(2)}) collective-permute-start(f32[4,1,128]{2,1,0:T(1,128)S(1)} %get-tuple-element.162), channel_id=1, source_target_pairs={{0,4},{4,8},{8,12},{1,5},{5,9},{9,13},{2,6},{6,10},{10,14},{3,7},{... | collective-permute-start | bytes 6152 | tf_op jit(solution)/shard_map/ppermute | solution.py:14
  36.3 16.4 %fusion.1 = f32[4,128,128]{2,0,1:T(4,128)S(1)} fusion(f32[128,128,128]{2,1,0:T(8,128)} %param.30, f32[128,4,128]{2,1,0:T(4,128)S(1)} %gather_fusion, f32[128,128]{1,0:T(8,128)S(1)} %broadcast_multiply_fusion, pred[128]{0:T(512)(128)(4,1)S(1)} %compare_and_fusion), kind=kOutput, calls=%fused_computation.5 | convolution fusion | flops 100794368 | bytes 8978560 | tf_op jit(solution)/shard_map/bij,pbj->pbi/dot_general | solution.py:92
  52.7 7.3 %fusion.92 = f32[128,4,128]{2,1,0:T(4,128)S(1)} fusion(f32[4,128,128]{2,0,1:T(4,128)S(1)} %fusion.1, f32[128,128,128]{2,1,0:T(8,128)S(1)} %copy-done), kind=kOutput, calls=%fused_computation.209 | convolution fusion | flops 100663296 | bytes 8912896 | tf_op jit(solution)/shard_map/bij,pbi->pbj/dot_general | solution.py:100
  60.6 3.5 %collective-permute-start.10 = (f32[4,384]{1,0:T(4,128)S(1)}, f32[4,384]{1,0:T(4,128)S(1)}, u32[]{:S(2)}, u32[]{:S(2)}) collective-permute-start(f32[4,384]{1,0:T(4,128)S(1)} %pad_maximum_fusion.74), channel_id=1, source_target_pairs={{0,4},{4,8},{8,12},{1,5},{5,9},{9,13},{2,6},{6,10},{10,14},{3,7},{... | collective-permute-start | bytes 18440 | tf_op jit(solution)/shard_map/ppermute | solution.py:25
  64.1 1.6 collective-permute-start.3
  65.7 1.5 collective-permute-start.2
  67.7 4.5 %collective-permute-done.2 = f32[4,34,1]{2,0,1:T(4,128)S(1)} collective-permute-done((f32[4,34,1]{2,0,1:T(4,128)S(1)}, f32[4,34,1]{2,0,1:T(4,128)S(1)}, u32[]{:S(2)}, u32[]{:S(2)}) %collective-permute-start.2) | collective-permute-done | bytes 576 | tf_op jit(solution)/shard_map/ppermute | solution.py:17
  72.4 1.3 collective-permute-start.4
  73.7 4.5 %collective-permute-start.5 = (f32[4,1,256]{2,0,1:T(4,128)S(1)}, f32[4,1,256]{2,0,1:T(4,128)S(1)}, u32[]{:S(2)}, u32[]{:S(2)}) collective-permute-start(f32[4,1,256]{2,0,1:T(4,128)S(1)} %get-tuple-element.144), channel_id=1, source_target_pairs={{0,4},{4,8},{8,12},{1,5},{5,9},{9,13},{2,6},{6,10},{10,14},{3,7},{... | collective-permute-start | bytes 12296 | tf_op jit(solution)/shard_map/ppermute | solution.py:14
  78.3 1.6 collective-permute-start.17
  79.9 1.3 collective-permute-start.16
  81.3 4.5 %collective-permute-start.7 = (f32[4,34,1]{2,0,1:T(4,128)S(1)}, f32[4,34,1]{2,0,1:T(4,128)S(1)}, u32[]{:S(2)}, u32[]{:S(2)}) collective-permute-start(f32[4,34,1]{2,0,1:T(4,128)S(1)} %get-tuple-element.135), channel_id=1, source_target_pairs={{0,2},{1,3},{4,6},{5,7},{8,10},{9,11},{12,14},{13,15},{16,18},{17,... | collective-permute-start | bytes 1640 | tf_op jit(solution)/shard_map/ppermute | solution.py:14
  85.9 1.3 collective-permute-start.6
  87.2 1.3 collective-permute-start.11
  88.6 4.2 %collective-permute-done.11 = f32[4,384]{1,0:T(4,128)S(1)} collective-permute-done((f32[4,384]{1,0:T(4,128)S(1)}, f32[4,384]{1,0:T(4,128)S(1)}, u32[]{:S(2)}, u32[]{:S(2)}) %collective-permute-start.11) | collective-permute-done | bytes 6176 | tf_op jit(solution)/shard_map/ppermute | solution.py:25
  93.5 19.8 %all-reduce = (f32[4]{0:T(128)S(1)}, f32[4]{0:T(128)S(1)}) all-reduce(f32[4]{0:T(128)S(1)} %add.192, f32[4]{0:T(128)S(1)} %add.213), channel_id=1, replica_groups=mesh['grp'=2,'ew'=4,'ns'=2,'lvl'=2] {'ew','ns'}, use_global_device_ids=true, to_apply=%region_2.0 | all-reduce | flops 8 | bytes 64 | tf_op jit(solution)/shard_map/psum | solution.py:77
  113.7 17.3 %psum.30 = f32[4]{0:T(128)S(1)} all-reduce(f32[4]{0:T(128)S(1)} %add.214), channel_id=1, replica_groups=mesh['grp'=2,'ew'=4,'ns'=2,'lvl'=2] {'ew','ns'}, use_global_device_ids=true, to_apply=%region_8.10 | all-reduce | flops 4 | bytes 32 | tf_op jit(solution)/shard_map/psum | solution.py:77
  131.3 1.3 collective-permute-start.27
  132.6 4.5 %collective-permute-start.26 = (f32[4,1,128]{2,1,0:T(1,128)S(1)}, f32[4,1,128]{2,1,0:T(1,128)S(1)}, u32[]{:S(2)}, u32[]{:S(2)}) collective-permute-start(f32[4,1,128]{2,1,0:T(1,128)S(1)} %get-tuple-element.160), channel_id=1, source_target_pairs={{0,4},{4,8},{8,12},{1,5},{5,9},{9,13},{2,6},{6,10},{10,14},{3,7},{... | collective-permute-start | bytes 6152 | tf_op jit(solution)/shard_map/ppermute | solution.py:14
  138.5 3.7 %collective-permute-start.31 = (f32[4,18,1]{2,1,0:T(8,128)S(1)}, f32[4,18,1]{2,1,0:T(8,128)S(1)}, u32[]{:S(2)}, u32[]{:S(2)}) collective-permute-start(f32[4,18,1]{2,1,0:T(8,128)S(1)} %get-tuple-element.151), channel_id=1, source_target_pairs={{0,2},{1,3},{4,6},{5,7},{8,10},{9,11},{12,14},{13,15},{16,18},{17,... | collective-permute-start | bytes 872 | tf_op jit(solution)/shard_map/ppermute | solution.py:14
  142.2 1.3 collective-permute-start.30
  143.5 1.3 collective-permute-start.18
  144.8 4.8 %collective-permute-start.19 = (f32[4,1,256]{2,0,1:T(4,128)S(1)}, f32[4,1,256]{2,0,1:T(4,128)S(1)}, u32[]{:S(2)}, u32[]{:S(2)}) collective-permute-start(f32[4,1,256]{2,0,1:T(4,128)S(1)} %get-tuple-element.142), channel_id=1, source_target_pairs={{0,4},{4,8},{8,12},{1,5},{5,9},{9,13},{2,6},{6,10},{10,14},{3,7},{... | collective-permute-start | bytes 12296 | tf_op jit(solution)/shard_map/ppermute | solution.py:14
  149.8 1.3 collective-permute-start.32
  151.1 4.6 %collective-permute-start.33 = (f32[4,1,128]{2,1,0:T(1,128)S(1)}, f32[4,1,128]{2,1,0:T(1,128)S(1)}, u32[]{:S(2)}, u32[]{:S(2)}) collective-permute-start(f32[4,1,128]{2,1,0:T(1,128)S(1)} %get-tuple-element.158), channel_id=1, source_target_pairs={{0,4},{4,8},{8,12},{1,5},{5,9},{9,13},{2,6},{6,10},{10,14},{3,7},{... | collective-permute-start | bytes 6152 | tf_op jit(solution)/shard_map/ppermute | solution.py:14
  156.5 15.5 %fusion = f32[4,128,128]{2,0,1:T(4,128)S(1)} fusion(f32[128,128,128]{2,1,0:T(8,128)} %param.30, f32[128,4,128]{2,1,0:T(4,128)S(1)} %gather_fusion.1, f32[128,128]{1,0:T(8,128)S(1)} %broadcast_multiply_fusion, pred[128]{0:T(512)(128)(4,1)S(1)} %compare_and_fusion), kind=kOutput, calls=%fused_computation.3 | convolution fusion | flops 100794368 | bytes 8978560 | tf_op jit(solution)/shard_map/bij,pbj->pbi/dot_general | solution.py:92
  172.0 9.4 %fusion.93 = f32[128,4,128]{2,1,0:T(4,128)S(1)} fusion(f32[4,128,128]{2,0,1:T(4,128)S(1)} %fusion, f32[128,128,128]{2,1,0:T(8,128)} %param.30), kind=kOutput, calls=%fused_computation.210 | convolution fusion | flops 100663296 | bytes 8912896 | tf_op jit(solution)/shard_map/bij,pbi->pbj/dot_general | solution.py:100
  181.9 3.9 %collective-permute-start.28 = (f32[4,384]{1,0:T(4,128)S(1)}, f32[4,384]{1,0:T(4,128)S(1)}, u32[]{:S(2)}, u32[]{:S(2)}) collective-permute-start(f32[4,384]{1,0:T(4,128)S(1)} %pad_maximum_fusion.76), channel_id=1, source_target_pairs={{0,4},{4,8},{8,12},{1,5},{5,9},{9,13},{2,6},{6,10},{10,14},{3,7},{... | collective-permute-start | bytes 18440 | tf_op jit(solution)/shard_map/ppermute | solution.py:25
  185.8 4.6 %collective-permute-start.21 = (f32[4,34,1]{2,0,1:T(4,128)S(1)}, f32[4,34,1]{2,0,1:T(4,128)S(1)}, u32[]{:S(2)}, u32[]{:S(2)}) collective-permute-start(f32[4,34,1]{2,0,1:T(4,128)S(1)} %get-tuple-element.131), channel_id=1, source_target_pairs={{0,2},{1,3},{4,6},{5,7},{8,10},{9,11},{12,14},{13,15},{16,18},{17,... | collective-permute-start | bytes 1640 | tf_op jit(solution)/shard_map/ppermute | solution.py:14
  190.4 1.3 collective-permute-start.20
  192.3 4.3 %collective-permute-done.20 = f32[4,34,1]{2,0,1:T(4,128)S(1)} collective-permute-done((f32[4,34,1]{2,0,1:T(4,128)S(1)}, f32[4,34,1]{2,0,1:T(4,128)S(1)}, u32[]{:S(2)}, u32[]{:S(2)}) %collective-permute-start.20) | collective-permute-done | bytes 576 | tf_op jit(solution)/shard_map/ppermute | solution.py:17
  196.8 1.3 collective-permute-start.22
  198.1 4.5 %collective-permute-start.23 = (f32[4,1,256]{2,0,1:T(4,128)S(1)}, f32[4,1,256]{2,0,1:T(4,128)S(1)}, u32[]{:S(2)}, u32[]{:S(2)}) collective-permute-start(f32[4,1,256]{2,0,1:T(4,128)S(1)} %get-tuple-element.140), channel_id=1, source_target_pairs={{0,4},{4,8},{8,12},{1,5},{5,9},{9,13},{2,6},{6,10},{10,14},{3,7},{... | collective-permute-start | bytes 12296 | tf_op jit(solution)/shard_map/ppermute | solution.py:14
  202.8 1.6 collective-permute-start.35
  204.3 1.3 collective-permute-start.34
  205.8 4.5 %collective-permute-start.25 = (f32[4,34,1]{2,0,1:T(4,128)S(1)}, f32[4,34,1]{2,0,1:T(4,128)S(1)}, u32[]{:S(2)}, u32[]{:S(2)}) collective-permute-start(f32[4,34,1]{2,0,1:T(4,128)S(1)} %get-tuple-element.129), channel_id=1, source_target_pairs={{0,2},{1,3},{4,6},{5,7},{8,10},{9,11},{12,14},{13,15},{16,18},{17,... | collective-permute-start | bytes 1640 | tf_op jit(solution)/shard_map/ppermute | solution.py:14
  210.4 1.3 collective-permute-start.24
  211.7 1.3 collective-permute-start.29
  213.0 4.2 %collective-permute-done.29 = f32[4,384]{1,0:T(4,128)S(1)} collective-permute-done((f32[4,384]{1,0:T(4,128)S(1)}, f32[4,384]{1,0:T(4,128)S(1)}, u32[]{:S(2)}, u32[]{:S(2)}) %collective-permute-start.29) | collective-permute-done | bytes 6176 | tf_op jit(solution)/shard_map/ppermute | solution.py:25
  217.9 19.8 %psum.31 = f32[4]{0:T(128)S(1)} all-reduce(f32[4]{0:T(128)S(1)} %add.235), channel_id=1, replica_groups=mesh['grp'=2,'ew'=4,'ns'=2,'lvl'=2] {'ew','ns'}, use_global_device_ids=true, to_apply=%region_11.13 | all-reduce | flops 4 | bytes 32 | tf_op jit(solution)/shard_map/psum | solution.py:124
  (138 shorter events, 16.5 us)
Async XLA Ops:
  1.4 18.1 %collective-permute-start.9 = (f32[4,1,128]{2,1,0:T(1,128)S(1)}, f32[4,1,128]{2,1,0:T(1,128)S(1)}, u32[]{:S(2)}, u32[]{:S(2)}) collective-permute-start(f32[4,1,128]{2,1,0:T(1,128)S(1)} %get-tuple-element.165), channel_id=1, source_target_pairs={{4,0},{8,4},{12,8},{5,1},{9,5},{13,9},{6,2},{10,6},{14,10},{7,3},{... | collective-permute-start | bytes 6152 | tf_op jit(solution)/shard_map/ppermute | solution.py:17
  2.7 16.8 %collective-permute-start.8 = (f32[4,1,128]{2,1,0:T(1,128)S(1)}, f32[4,1,128]{2,1,0:T(1,128)S(1)}, u32[]{:S(2)}, u32[]{:S(2)}) collective-permute-start(f32[4,1,128]{2,1,0:T(1,128)S(1)} %get-tuple-element.164), channel_id=1, source_target_pairs={{0,4},{4,8},{8,12},{1,5},{5,9},{9,13},{2,6},{6,10},{10,14},{3,7},{... | collective-permute-start | bytes 6152 | tf_op jit(solution)/shard_map/ppermute | solution.py:14
  9.3 26.1 %collective-permute-start = (f32[4,1,256]{2,0,1:T(4,128)S(1)}, f32[4,1,256]{2,0,1:T(4,128)S(1)}, u32[]{:S(2)}, u32[]{:S(2)}) collective-permute-start(f32[4,1,256]{2,0,1:T(4,128)S(1)} %get-tuple-element.147), channel_id=1, source_target_pairs={{4,0},{8,4},{12,8},{5,1},{9,5},{13,9},{6,2},{10,6},{14,10},{7,3},{... | collective-permute-start | bytes 12296 | tf_op jit(solution)/shard_map/ppermute | solution.py:17
  10.6 24.8 %collective-permute-start.1 = (f32[4,1,256]{2,0,1:T(4,128)S(1)}, f32[4,1,256]{2,0,1:T(4,128)S(1)}, u32[]{:S(2)}, u32[]{:S(2)}) collective-permute-start(f32[4,1,256]{2,0,1:T(4,128)S(1)} %get-tuple-element.146), channel_id=1, source_target_pairs={{0,4},{4,8},{8,12},{1,5},{5,9},{9,13},{2,6},{6,10},{10,14},{3,7},{... | collective-permute-start | bytes 12296 | tf_op jit(solution)/shard_map/ppermute | solution.py:14
  19.6 5.6 %collective-permute-start.13 = (f32[4,18,1]{2,1,0:T(8,128)S(1)}, f32[4,18,1]{2,1,0:T(8,128)S(1)}, u32[]{:S(2)}, u32[]{:S(2)}) collective-permute-start(f32[4,18,1]{2,1,0:T(8,128)S(1)} %get-tuple-element.155), channel_id=1, source_target_pairs={{0,2},{1,3},{4,6},{5,7},{8,10},{9,11},{12,14},{13,15},{16,18},{17,... | collective-permute-start | bytes 872 | tf_op jit(solution)/shard_map/ppermute | solution.py:14
  23.5 6.0 %collective-permute-start.12 = (f32[4,18,1]{2,1,0:T(8,128)S(1)}, f32[4,18,1]{2,1,0:T(8,128)S(1)}, u32[]{:S(2)}, u32[]{:S(2)}) collective-permute-start(f32[4,18,1]{2,1,0:T(8,128)S(1)} %get-tuple-element.154), channel_id=1, source_target_pairs={{2,0},{3,1},{6,4},{7,5},{10,8},{11,9},{14,12},{15,13},{18,16},{19,... | collective-permute-start | bytes 872 | tf_op jit(solution)/shard_map/ppermute | solution.py:17
  29.6 37.6 %collective-permute-start.14 = (f32[4,1,128]{2,1,0:T(1,128)S(1)}, f32[4,1,128]{2,1,0:T(1,128)S(1)}, u32[]{:S(2)}, u32[]{:S(2)}) collective-permute-start(f32[4,1,128]{2,1,0:T(1,128)S(1)} %get-tuple-element.163), channel_id=1, source_target_pairs={{4,0},{8,4},{12,8},{5,1},{9,5},{13,9},{6,2},{10,6},{14,10},{7,3},{... | collective-permute-start | bytes 6152 | tf_op jit(solution)/shard_map/ppermute | solution.py:17
  30.9 36.4 %collective-permute-start.15 = (f32[4,1,128]{2,1,0:T(1,128)S(1)}, f32[4,1,128]{2,1,0:T(1,128)S(1)}, u32[]{:S(2)}, u32[]{:S(2)}) collective-permute-start(f32[4,1,128]{2,1,0:T(1,128)S(1)} %get-tuple-element.162), channel_id=1, source_target_pairs={{0,4},{4,8},{8,12},{1,5},{5,9},{9,13},{2,6},{6,10},{10,14},{3,7},{... | collective-permute-start | bytes 6152 | tf_op jit(solution)/shard_map/ppermute | solution.py:14
  36.3 16.4 %copy-start = (f32[128,128,128]{2,1,0:T(8,128)S(1)}, f32[128,128,128]{2,1,0:T(8,128)}, u32[]{:S(2)}) copy-start(f32[128,128,128]{2,1,0:T(8,128)} %param.30) | copy-start | bytes 25165828
  36.3 23.7 %copy-start.3 = (s32[128]{0:T(128)S(1)}, s32[128]{0:T(128)}, u32[]{:S(2)}) copy-start(s32[128]{0:T(128)} %param.32) | copy-start | bytes 1540
  36.3 56.5 %copy-start.1 = (s32[4,32,256]{2,1,0:T(8,128)S(1)}, s32[4,32,256]{2,1,0:T(8,128)}, u32[]{:S(2)}) copy-start(s32[4,32,256]{2,1,0:T(8,128)} %param.26) | copy-start | bytes 393220
  52.7 40.5 %copy-start.2 = (s32[4,16,128]{2,1,0:T(8,128)S(1)}, s32[4,16,128]{2,1,0:T(8,128)}, u32[]{:S(2)}) copy-start(s32[4,16,128]{2,1,0:T(8,128)} %param.27) | copy-start | bytes 98308
  60.6 26.6 %collective-permute-start.10 = (f32[4,384]{1,0:T(4,128)S(1)}, f32[4,384]{1,0:T(4,128)S(1)}, u32[]{:S(2)}, u32[]{:S(2)}) collective-permute-start(f32[4,384]{1,0:T(4,128)S(1)} %pad_maximum_fusion.74), channel_id=1, source_target_pairs={{0,4},{4,8},{8,12},{1,5},{5,9},{9,13},{2,6},{6,10},{10,14},{3,7},{... | collective-permute-start | bytes 18440 | tf_op jit(solution)/shard_map/ppermute | solution.py:25
  64.1 3.5 %collective-permute-start.3 = (f32[4,34,1]{2,0,1:T(4,128)S(1)}, f32[4,34,1]{2,0,1:T(4,128)S(1)}, u32[]{:S(2)}, u32[]{:S(2)}) collective-permute-start(f32[4,34,1]{2,0,1:T(4,128)S(1)} %get-tuple-element.137), channel_id=1, source_target_pairs={{0,2},{1,3},{4,6},{5,7},{8,10},{9,11},{12,14},{13,15},{16,18},{17,... | collective-permute-start | bytes 1640 | tf_op jit(solution)/shard_map/ppermute | solution.py:14
  65.7 6.4 %collective-permute-start.2 = (f32[4,34,1]{2,0,1:T(4,128)S(1)}, f32[4,34,1]{2,0,1:T(4,128)S(1)}, u32[]{:S(2)}, u32[]{:S(2)}) collective-permute-start(f32[4,34,1]{2,0,1:T(4,128)S(1)} %get-tuple-element.136), channel_id=1, source_target_pairs={{2,0},{3,1},{6,4},{7,5},{10,8},{11,9},{14,12},{15,13},{18,16},{19,... | collective-permute-start | bytes 1640 | tf_op jit(solution)/shard_map/ppermute | solution.py:17
  72.4 8.8 %collective-permute-start.4 = (f32[4,1,256]{2,0,1:T(4,128)S(1)}, f32[4,1,256]{2,0,1:T(4,128)S(1)}, u32[]{:S(2)}, u32[]{:S(2)}) collective-permute-start(f32[4,1,256]{2,0,1:T(4,128)S(1)} %get-tuple-element.145), channel_id=1, source_target_pairs={{4,0},{8,4},{12,8},{5,1},{9,5},{13,9},{6,2},{10,6},{14,10},{7,3},{... | collective-permute-start | bytes 12296 | tf_op jit(solution)/shard_map/ppermute | solution.py:17
  73.7 7.5 %collective-permute-start.5 = (f32[4,1,256]{2,0,1:T(4,128)S(1)}, f32[4,1,256]{2,0,1:T(4,128)S(1)}, u32[]{:S(2)}, u32[]{:S(2)}) collective-permute-start(f32[4,1,256]{2,0,1:T(4,128)S(1)} %get-tuple-element.144), channel_id=1, source_target_pairs={{0,4},{4,8},{8,12},{1,5},{5,9},{9,13},{2,6},{6,10},{10,14},{3,7},{... | collective-permute-start | bytes 12296 | tf_op jit(solution)/shard_map/ppermute | solution.py:14
  78.3 14.9 %collective-permute-start.17 = (f32[4,18,1]{2,1,0:T(8,128)S(1)}, f32[4,18,1]{2,1,0:T(8,128)S(1)}, u32[]{:S(2)}, u32[]{:S(2)}) collective-permute-start(f32[4,18,1]{2,1,0:T(8,128)S(1)} %get-tuple-element.153), channel_id=1, source_target_pairs={{0,2},{1,3},{4,6},{5,7},{8,10},{9,11},{12,14},{13,15},{16,18},{17,... | collective-permute-start | bytes 872 | tf_op jit(solution)/shard_map/ppermute | solution.py:14
  79.9 13.4 %collective-permute-start.16 = (f32[4,18,1]{2,1,0:T(8,128)S(1)}, f32[4,18,1]{2,1,0:T(8,128)S(1)}, u32[]{:S(2)}, u32[]{:S(2)}) collective-permute-start(f32[4,18,1]{2,1,0:T(8,128)S(1)} %get-tuple-element.152), channel_id=1, source_target_pairs={{2,0},{3,1},{6,4},{7,5},{10,8},{11,9},{14,12},{15,13},{18,16},{19,... | collective-permute-start | bytes 872 | tf_op jit(solution)/shard_map/ppermute | solution.py:17
  81.3 11.4 %collective-permute-start.7 = (f32[4,34,1]{2,0,1:T(4,128)S(1)}, f32[4,34,1]{2,0,1:T(4,128)S(1)}, u32[]{:S(2)}, u32[]{:S(2)}) collective-permute-start(f32[4,34,1]{2,0,1:T(4,128)S(1)} %get-tuple-element.135), channel_id=1, source_target_pairs={{0,2},{1,3},{4,6},{5,7},{8,10},{9,11},{12,14},{13,15},{16,18},{17,... | collective-permute-start | bytes 1640 | tf_op jit(solution)/shard_map/ppermute | solution.py:14
  85.9 6.9 %collective-permute-start.6 = (f32[4,34,1]{2,0,1:T(4,128)S(1)}, f32[4,34,1]{2,0,1:T(4,128)S(1)}, u32[]{:S(2)}, u32[]{:S(2)}) collective-permute-start(f32[4,34,1]{2,0,1:T(4,128)S(1)} %get-tuple-element.134), channel_id=1, source_target_pairs={{2,0},{3,1},{6,4},{7,5},{10,8},{11,9},{14,12},{15,13},{18,16},{19,... | collective-permute-start | bytes 1640 | tf_op jit(solution)/shard_map/ppermute | solution.py:17
  87.2 5.5 %collective-permute-start.11 = (f32[4,384]{1,0:T(4,128)S(1)}, f32[4,384]{1,0:T(4,128)S(1)}, u32[]{:S(2)}, u32[]{:S(2)}) collective-permute-start(f32[4,384]{1,0:T(4,128)S(1)} %pad_maximum_fusion.75), channel_id=1, source_target_pairs={{4,0},{8,4},{12,8},{5,1},{9,5},{13,9},{6,2},{10,6},{14,10},{7,3},{... | collective-permute-start | bytes 18440 | tf_op jit(solution)/shard_map/ppermute | solution.py:25
  131.3 5.9 %collective-permute-start.27 = (f32[4,1,128]{2,1,0:T(1,128)S(1)}, f32[4,1,128]{2,1,0:T(1,128)S(1)}, u32[]{:S(2)}, u32[]{:S(2)}) collective-permute-start(f32[4,1,128]{2,1,0:T(1,128)S(1)} %get-tuple-element.161), channel_id=1, source_target_pairs={{4,0},{8,4},{12,8},{5,1},{9,5},{13,9},{6,2},{10,6},{14,10},{7,3},{... | collective-permute-start | bytes 6152 | tf_op jit(solution)/shard_map/ppermute | solution.py:17
  132.6 5.8 %collective-permute-start.26 = (f32[4,1,128]{2,1,0:T(1,128)S(1)}, f32[4,1,128]{2,1,0:T(1,128)S(1)}, u32[]{:S(2)}, u32[]{:S(2)}) collective-permute-start(f32[4,1,128]{2,1,0:T(1,128)S(1)} %get-tuple-element.160), channel_id=1, source_target_pairs={{0,4},{4,8},{8,12},{1,5},{5,9},{9,13},{2,6},{6,10},{10,14},{3,7},{... | collective-permute-start | bytes 6152 | tf_op jit(solution)/shard_map/ppermute | solution.py:14
  138.5 11.1 %collective-permute-start.31 = (f32[4,18,1]{2,1,0:T(8,128)S(1)}, f32[4,18,1]{2,1,0:T(8,128)S(1)}, u32[]{:S(2)}, u32[]{:S(2)}) collective-permute-start(f32[4,18,1]{2,1,0:T(8,128)S(1)} %get-tuple-element.151), channel_id=1, source_target_pairs={{0,2},{1,3},{4,6},{5,7},{8,10},{9,11},{12,14},{13,15},{16,18},{17,... | collective-permute-start | bytes 872 | tf_op jit(solution)/shard_map/ppermute | solution.py:14
  142.2 7.4 %collective-permute-start.30 = (f32[4,18,1]{2,1,0:T(8,128)S(1)}, f32[4,18,1]{2,1,0:T(8,128)S(1)}, u32[]{:S(2)}, u32[]{:S(2)}) collective-permute-start(f32[4,18,1]{2,1,0:T(8,128)S(1)} %get-tuple-element.150), channel_id=1, source_target_pairs={{2,0},{3,1},{6,4},{7,5},{10,8},{11,9},{14,12},{15,13},{18,16},{19,... | collective-permute-start | bytes 872 | tf_op jit(solution)/shard_map/ppermute | solution.py:17
  143.5 12.1 %collective-permute-start.18 = (f32[4,1,256]{2,0,1:T(4,128)S(1)}, f32[4,1,256]{2,0,1:T(4,128)S(1)}, u32[]{:S(2)}, u32[]{:S(2)}) collective-permute-start(f32[4,1,256]{2,0,1:T(4,128)S(1)} %get-tuple-element.143), channel_id=1, source_target_pairs={{4,0},{8,4},{12,8},{5,1},{9,5},{13,9},{6,2},{10,6},{14,10},{7,3},{... | collective-permute-start | bytes 12296 | tf_op jit(solution)/shard_map/ppermute | solution.py:17
  144.8 10.8 %collective-permute-start.19 = (f32[4,1,256]{2,0,1:T(4,128)S(1)}, f32[4,1,256]{2,0,1:T(4,128)S(1)}, u32[]{:S(2)}, u32[]{:S(2)}) collective-permute-start(f32[4,1,256]{2,0,1:T(4,128)S(1)} %get-tuple-element.142), channel_id=1, source_target_pairs={{0,4},{4,8},{8,12},{1,5},{5,9},{9,13},{2,6},{6,10},{10,14},{3,7},{... | collective-permute-start | bytes 12296 | tf_op jit(solution)/shard_map/ppermute | solution.py:14
  149.8 41.9 %collective-permute-start.32 = (f32[4,1,128]{2,1,0:T(1,128)S(1)}, f32[4,1,128]{2,1,0:T(1,128)S(1)}, u32[]{:S(2)}, u32[]{:S(2)}) collective-permute-start(f32[4,1,128]{2,1,0:T(1,128)S(1)} %get-tuple-element.159), channel_id=1, source_target_pairs={{4,0},{8,4},{12,8},{5,1},{9,5},{13,9},{6,2},{10,6},{14,10},{7,3},{... | collective-permute-start | bytes 6152 | tf_op jit(solution)/shard_map/ppermute | solution.py:17
  151.1 40.6 %collective-permute-start.33 = (f32[4,1,128]{2,1,0:T(1,128)S(1)}, f32[4,1,128]{2,1,0:T(1,128)S(1)}, u32[]{:S(2)}, u32[]{:S(2)}) collective-permute-start(f32[4,1,128]{2,1,0:T(1,128)S(1)} %get-tuple-element.158), channel_id=1, source_target_pairs={{0,4},{4,8},{8,12},{1,5},{5,9},{9,13},{2,6},{6,10},{10,14},{3,7},{... | collective-permute-start | bytes 6152 | tf_op jit(solution)/shard_map/ppermute | solution.py:14
  181.9 29.8 %collective-permute-start.28 = (f32[4,384]{1,0:T(4,128)S(1)}, f32[4,384]{1,0:T(4,128)S(1)}, u32[]{:S(2)}, u32[]{:S(2)}) collective-permute-start(f32[4,384]{1,0:T(4,128)S(1)} %pad_maximum_fusion.76), channel_id=1, source_target_pairs={{0,4},{4,8},{8,12},{1,5},{5,9},{9,13},{2,6},{6,10},{10,14},{3,7},{... | collective-permute-start | bytes 18440 | tf_op jit(solution)/shard_map/ppermute | solution.py:25
  185.8 6.5 %collective-permute-start.21 = (f32[4,34,1]{2,0,1:T(4,128)S(1)}, f32[4,34,1]{2,0,1:T(4,128)S(1)}, u32[]{:S(2)}, u32[]{:S(2)}) collective-permute-start(f32[4,34,1]{2,0,1:T(4,128)S(1)} %get-tuple-element.131), channel_id=1, source_target_pairs={{0,2},{1,3},{4,6},{5,7},{8,10},{9,11},{12,14},{13,15},{16,18},{17,... | collective-permute-start | bytes 1640 | tf_op jit(solution)/shard_map/ppermute | solution.py:14
  190.4 6.2 %collective-permute-start.20 = (f32[4,34,1]{2,0,1:T(4,128)S(1)}, f32[4,34,1]{2,0,1:T(4,128)S(1)}, u32[]{:S(2)}, u32[]{:S(2)}) collective-permute-start(f32[4,34,1]{2,0,1:T(4,128)S(1)} %get-tuple-element.130), channel_id=1, source_target_pairs={{2,0},{3,1},{6,4},{7,5},{10,8},{11,9},{14,12},{15,13},{18,16},{19,... | collective-permute-start | bytes 1640 | tf_op jit(solution)/shard_map/ppermute | solution.py:17
  196.8 8.8 %collective-permute-start.22 = (f32[4,1,256]{2,0,1:T(4,128)S(1)}, f32[4,1,256]{2,0,1:T(4,128)S(1)}, u32[]{:S(2)}, u32[]{:S(2)}) collective-permute-start(f32[4,1,256]{2,0,1:T(4,128)S(1)} %get-tuple-element.141), channel_id=1, source_target_pairs={{4,0},{8,4},{12,8},{5,1},{9,5},{13,9},{6,2},{10,6},{14,10},{7,3},{... | collective-permute-start | bytes 12296 | tf_op jit(solution)/shard_map/ppermute | solution.py:17
  198.1 7.5 %collective-permute-start.23 = (f32[4,1,256]{2,0,1:T(4,128)S(1)}, f32[4,1,256]{2,0,1:T(4,128)S(1)}, u32[]{:S(2)}, u32[]{:S(2)}) collective-permute-start(f32[4,1,256]{2,0,1:T(4,128)S(1)} %get-tuple-element.140), channel_id=1, source_target_pairs={{0,4},{4,8},{8,12},{1,5},{5,9},{9,13},{2,6},{6,10},{10,14},{3,7},{... | collective-permute-start | bytes 12296 | tf_op jit(solution)/shard_map/ppermute | solution.py:14
  202.8 14.9 %collective-permute-start.35 = (f32[4,18,1]{2,1,0:T(8,128)S(1)}, f32[4,18,1]{2,1,0:T(8,128)S(1)}, u32[]{:S(2)}, u32[]{:S(2)}) collective-permute-start(f32[4,18,1]{2,1,0:T(8,128)S(1)} %get-tuple-element.149), channel_id=1, source_target_pairs={{0,2},{1,3},{4,6},{5,7},{8,10},{9,11},{12,14},{13,15},{16,18},{17,... | collective-permute-start | bytes 872 | tf_op jit(solution)/shard_map/ppermute | solution.py:14
  204.3 13.3 %collective-permute-start.34 = (f32[4,18,1]{2,1,0:T(8,128)S(1)}, f32[4,18,1]{2,1,0:T(8,128)S(1)}, u32[]{:S(2)}, u32[]{:S(2)}) collective-permute-start(f32[4,18,1]{2,1,0:T(8,128)S(1)} %get-tuple-element.148), channel_id=1, source_target_pairs={{2,0},{3,1},{6,4},{7,5},{10,8},{11,9},{14,12},{15,13},{18,16},{19,... | collective-permute-start | bytes 872 | tf_op jit(solution)/shard_map/ppermute | solution.py:17
  205.8 11.4 %collective-permute-start.25 = (f32[4,34,1]{2,0,1:T(4,128)S(1)}, f32[4,34,1]{2,0,1:T(4,128)S(1)}, u32[]{:S(2)}, u32[]{:S(2)}) collective-permute-start(f32[4,34,1]{2,0,1:T(4,128)S(1)} %get-tuple-element.129), channel_id=1, source_target_pairs={{0,2},{1,3},{4,6},{5,7},{8,10},{9,11},{12,14},{13,15},{16,18},{17,... | collective-permute-start | bytes 1640 | tf_op jit(solution)/shard_map/ppermute | solution.py:14
  210.4 6.9 %collective-permute-start.24 = (f32[4,34,1]{2,0,1:T(4,128)S(1)}, f32[4,34,1]{2,0,1:T(4,128)S(1)}, u32[]{:S(2)}, u32[]{:S(2)}) collective-permute-start(f32[4,34,1]{2,0,1:T(4,128)S(1)} %get-tuple-element.128), channel_id=1, source_target_pairs={{2,0},{3,1},{6,4},{7,5},{10,8},{11,9},{14,12},{15,13},{18,16},{19,... | collective-permute-start | bytes 1640 | tf_op jit(solution)/shard_map/ppermute | solution.py:17
  211.7 5.5 %collective-permute-start.29 = (f32[4,384]{1,0:T(4,128)S(1)}, f32[4,384]{1,0:T(4,128)S(1)}, u32[]{:S(2)}, u32[]{:S(2)}) collective-permute-start(f32[4,384]{1,0:T(4,128)S(1)} %pad_maximum_fusion.77), channel_id=1, source_target_pairs={{4,0},{8,4},{12,8},{5,1},{9,5},{13,9},{6,2},{10,6},{14,10},{7,3},{... | collective-permute-start | bytes 18440 | tf_op jit(solution)/shard_map/ppermute | solution.py:25
where the time goes:
time: 241 us; the launch traced here: 240 us
  starting transfers between devices  94.4 us (39%)
  blocking collectives  56.9 us (24%)
  matrix products  49 us (20%)
  waiting for transfers between devices  24 us (10%)
  other arithmetic  9.25 us (4%)
  local copies, waits for them, and re-layouts  4.04 us (2%)
    ppermute x16, starting transfers between devices, with_halo(): lax.ppermute(lax.slice_in_dim(block, block.shape[dim] - width, None, axis...  63.6 us
    psum x2, blocking collectives, squares(): lax.psum(local_products(first_fine, first_coarse, first_fine, first_coars...  37.1 us
    dot_general x2, matrix products, local(): jnp.einsum('bij,pbj->pbi', phi_tiles, picked, precision=lax.Precision.HIG...  31.8 us
    ppermute x16, starting transfers between devices, with_halo(): lax.ppermute(lax.slice_in_dim(block, 0, width, axis=dim), axis, backward)  20.9 us
    psum x1, blocking collectives, local(): lax.psum(local_products(direction_fine, direction_coarse, image_fine, ima...  19.8 us
    dot_general x2, matrix products, local(): jnp.einsum('bij,pbi->pbj', phi_tiles, scaled, precision=lax.Precision.HIG...  16.7 us
    ppermute x16, waiting for transfers between devices, with_halo(): lax.ppermute(lax.slice_in_dim(block, 0, width, axis=dim), axis, backward)  13 us
    ppermute x4, starting transfers between devices, shifted(): return lax.ppermute(block, axis, route)  9.99 us
  transfers between devices with their start and end apart: 36, of which 9 were waited for; matrix products, arithmetic and copies ran while one was open for 24% of the time, Pallas kernels for 0%

commit v1 on v0

--- a/solution.py
+++ b/solution.py
@@ -121,9 +121,9 @@
         )
         image_fine = prior_fine + inner_fine
         image_coarse = prior_coarse + inner_coarse
-        curve = lax.psum(
-            local_products(direction_fine, direction_coarse, image_fine, image_coarse), ("ew", "ns")
-        )
+        curve = local_products(direction_fine, direction_coarse, image_fine, image_coarse)
+        for name in ("ns", "ew"):
+            curve = lax.psum(curve, name)
         alpha = (norm_now / curve)[:, None, None]
         solve_fine = solve_fine + alpha * direction_fine
         solve_coarse = solve_coarse + alpha * direction_coarse

time: 241 us -> 249 us (1.033)
  blocking collectives: 56.9 us -> 65.5 us
    psum x1 -> x4, blocking collectives: 19.8 us -> 27.8 us  [local(): curve = lax.psum(curve, name)]
  transfers between devices with their start and end apart: 36 -> 36, of which waited for: 9 -> 9; matrix products, arithmetic and copies ran while one was open for 24% -> 23% of each run, Pallas kernels for 0% -> 0%
where the time goes in v1:
time: 249 us; the launch traced here: 247 us
  starting transfers between devices  93.2 us (37%)
  blocking collectives  65.5 us (26%)
  matrix products  49 us (20%)
  waiting for transfers between devices  24 us (10%)
  other arithmetic  9.25 us (4%)
  local copies, waits for them, and re-layouts  4.04 us (2%)
    ppermute x16, starting transfers between devices, with_halo(): lax.ppermute(lax.slice_in_dim(block, block.shape[dim] - width, None, axis...  62.3 us
    psum x2, blocking collectives, squares(): lax.psum(local_products(first_fine, first_coarse, first_fine, first_coars...  37.7 us
    dot_general x2, matrix products, local(): jnp.einsum('bij,pbj->pbi', phi_tiles, picked, precision=lax.Precision.HIG...  31.8 us
    psum x4, blocking collectives, local(): curve = lax.psum(curve, name)  27.8 us
    ppermute x16, starting transfers between devices, with_halo(): lax.ppermute(lax.slice_in_dim(block, 0, width, axis=dim), axis, backward)  20.9 us
    dot_general x2, matrix products, local(): jnp.einsum('bij,pbi->pbj', phi_tiles, scaled, precision=lax.Precision.HIG...  16.7 us
    ppermute x16, waiting for transfers between devices, with_halo(): lax.ppermute(lax.slice_in_dim(block, 0, width, axis=dim), axis, backward)  13 us
    ppermute x4, starting transfers between devices, shifted(): return lax.ppermute(block, axis, route)  9.98 us
  transfers between devices with their start and end apart: 36, of which 9 were waited for; matrix products, arithmetic and copies ran while one was open for 23% of the time, Pallas kernels for 0%

profile of v1, /device:TPU:0, one launch (start us, length us, event | category | flops | bytes accessed | tf_op | source)
XLA Modules:
  0.0 247.3 jit_solution(13502533659622694613)
XLA Ops:
  1.4 1.3 collective-permute-start.9
  2.7 5.6 %collective-permute-start.8 = (f32[4,1,128]{2,1,0:T(1,128)S(1)}, f32[4,1,128]{2,1,0:T(1,128)S(1)}, u32[]{:S(2)}, u32[]{:S(2)}) collective-permute-start(f32[4,1,128]{2,1,0:T(1,128)S(1)} %get-tuple-element.162), channel_id=1, source_target_pairs={{0,4},{4,8},{8,12},{1,5},{5,9},{9,13},{2,6},{6,10},{10,14},{3,7},{... | collective-permute-start | bytes 6152 | tf_op jit(solution)/shard_map/ppermute | solution.py:14
  9.3 1.3 collective-permute-start
  10.6 4.6 %collective-permute-start.1 = (f32[4,1,256]{2,0,1:T(4,128)S(1)}, f32[4,1,256]{2,0,1:T(4,128)S(1)}, u32[]{:S(2)}, u32[]{:S(2)}) collective-permute-start(f32[4,1,256]{2,0,1:T(4,128)S(1)} %get-tuple-element.144), channel_id=1, source_target_pairs={{0,4},{4,8},{8,12},{1,5},{5,9},{9,13},{2,6},{6,10},{10,14},{3,7},{... | collective-permute-start | bytes 12296 | tf_op jit(solution)/shard_map/ppermute | solution.py:14
  19.6 3.8 %collective-permute-start.13 = (f32[4,18,1]{2,1,0:T(8,128)S(1)}, f32[4,18,1]{2,1,0:T(8,128)S(1)}, u32[]{:S(2)}, u32[]{:S(2)}) collective-permute-start(f32[4,18,1]{2,1,0:T(8,128)S(1)} %get-tuple-element.153), channel_id=1, source_target_pairs={{0,2},{1,3},{4,6},{5,7},{8,10},{9,11},{12,14},{13,15},{16,18},{17,... | collective-permute-start | bytes 872 | tf_op jit(solution)/shard_map/ppermute | solution.py:14
  23.5 1.3 collective-permute-start.12
  25.2 4.3 %collective-permute-done.12 = f32[4,18,1]{2,1,0:T(8,128)S(1)} collective-permute-done((f32[4,18,1]{2,1,0:T(8,128)S(1)}, f32[4,18,1]{2,1,0:T(8,128)S(1)}, u32[]{:S(2)}, u32[]{:S(2)}) %collective-permute-start.12) | collective-permute-done | bytes 320 | tf_op jit(solution)/shard_map/ppermute | solution.py:17
  29.6 1.3 collective-permute-start.14
  30.9 4.5 %collective-permute-start.15 = (f32[4,1,128]{2,1,0:T(1,128)S(1)}, f32[4,1,128]{2,1,0:T(1,128)S(1)}, u32[]{:S(2)}, u32[]{:S(2)}) collective-permute-start(f32[4,1,128]{2,1,0:T(1,128)S(1)} %get-tuple-element.160), channel_id=1, source_target_pairs={{0,4},{4,8},{8,12},{1,5},{5,9},{9,13},{2,6},{6,10},{10,14},{3,7},{... | collective-permute-start | bytes 6152 | tf_op jit(solution)/shard_map/ppermute | solution.py:14
  36.3 16.4 %fusion.1 = f32[4,128,128]{2,0,1:T(4,128)S(1)} fusion(f32[128,128,128]{2,1,0:T(8,128)} %param.30, f32[128,4,128]{2,1,0:T(4,128)S(1)} %gather_fusion, f32[128,128]{1,0:T(8,128)S(1)} %broadcast_multiply_fusion, pred[128]{0:T(512)(128)(4,1)S(1)} %compare_and_fusion), kind=kOutput, calls=%fused_computation.5 | convolution fusion | flops 100794368 | bytes 8978560 | tf_op jit(solution)/shard_map/bij,pbj->pbi/dot_general | solution.py:92
  52.7 7.3 %fusion.92 = f32[128,4,128]{2,1,0:T(4,128)S(1)} fusion(f32[4,128,128]{2,0,1:T(4,128)S(1)} %fusion.1, f32[128,128,128]{2,1,0:T(8,128)S(1)} %copy-done), kind=kOutput, calls=%fused_computation.209 | convolution fusion | flops 100663296 | bytes 8912896 | tf_op jit(solution)/shard_map/bij,pbi->pbj/dot_general | solution.py:100
  60.6 3.5 %collective-permute-start.10 = (f32[4,384]{1,0:T(4,128)S(1)}, f32[4,384]{1,0:T(4,128)S(1)}, u32[]{:S(2)}, u32[]{:S(2)}) collective-permute-start(f32[4,384]{1,0:T(4,128)S(1)} %pad_maximum_fusion.74), channel_id=1, source_target_pairs={{0,4},{4,8},{8,12},{1,5},{5,9},{9,13},{2,6},{6,10},{10,14},{3,7},{... | collective-permute-start | bytes 18440 | tf_op jit(solution)/shard_map/ppermute | solution.py:25
  64.1 1.6 collective-permute-start.3
  65.7 1.5 collective-permute-start.2
  67.7 4.5 %collective-permute-done.2 = f32[4,34,1]{2,0,1:T(4,128)S(1)} collective-permute-done((f32[4,34,1]{2,0,1:T(4,128)S(1)}, f32[4,34,1]{2,0,1:T(4,128)S(1)}, u32[]{:S(2)}, u32[]{:S(2)}) %collective-permute-start.2) | collective-permute-done | bytes 576 | tf_op jit(solution)/shard_map/ppermute | solution.py:17
  72.4 1.3 collective-permute-start.4
  73.7 4.5 %collective-permute-start.5 = (f32[4,1,256]{2,0,1:T(4,128)S(1)}, f32[4,1,256]{2,0,1:T(4,128)S(1)}, u32[]{:S(2)}, u32[]{:S(2)}) collective-permute-start(f32[4,1,256]{2,0,1:T(4,128)S(1)} %get-tuple-element.142), channel_id=1, source_target_pairs={{0,4},{4,8},{8,12},{1,5},{5,9},{9,13},{2,6},{6,10},{10,14},{3,7},{... | collective-permute-start | bytes 12296 | tf_op jit(solution)/shard_map/ppermute | solution.py:14
  78.3 1.6 collective-permute-start.17
  79.9 1.3 collective-permute-start.16
  81.3 4.5 %collective-permute-start.7 = (f32[4,34,1]{2,0,1:T(4,128)S(1)}, f32[4,34,1]{2,0,1:T(4,128)S(1)}, u32[]{:S(2)}, u32[]{:S(2)}) collective-permute-start(f32[4,34,1]{2,0,1:T(4,128)S(1)} %get-tuple-element.133), channel_id=1, source_target_pairs={{0,2},{1,3},{4,6},{5,7},{8,10},{9,11},{12,14},{13,15},{16,18},{17,... | collective-permute-start | bytes 1640 | tf_op jit(solution)/shard_map/ppermute | solution.py:14
  85.9 1.3 collective-permute-start.6
  87.2 1.3 collective-permute-start.11
  88.6 4.2 %collective-permute-done.11 = f32[4,384]{1,0:T(4,128)S(1)} collective-permute-done((f32[4,384]{1,0:T(4,128)S(1)}, f32[4,384]{1,0:T(4,128)S(1)}, u32[]{:S(2)}, u32[]{:S(2)}) %collective-permute-start.11) | collective-permute-done | bytes 6176 | tf_op jit(solution)/shard_map/ppermute | solution.py:25
  93.5 5.5 %psum.43 = f32[4]{0:T(128)S(1)} all-reduce(f32[4]{0:T(128)S(1)} %add.217), channel_id=1, replica_groups=mesh['grp'=2,'ew'=4,'ns'=2,'lvl'=2] {'ns'}, use_global_device_ids=true, to_apply=%region_5.7 | all-reduce | flops 4 | bytes 32 | tf_op jit(solution)/shard_map/psum | solution.py:126
  99.0 19.1 %psum.42 = f32[4]{0:T(128)S(1)} all-reduce(f32[4]{0:T(128)S(1)} %add.196), channel_id=1, replica_groups=mesh['grp'=2,'ew'=4,'ns'=2,'lvl'=2] {'ew','ns'}, use_global_device_ids=true, to_apply=%region_2.0 | all-reduce | flops 4 | bytes 32 | tf_op jit(solution)/shard_map/psum | solution.py:77
  118.2 8.4 %psum.44 = f32[4]{0:T(128)S(1)} all-reduce(f32[4]{0:T(128)S(1)} %psum.43), channel_id=1, replica_groups=mesh['grp'=2,'ew'=4,'ns'=2,'lvl'=2] {'ew'}, use_global_device_ids=true, to_apply=%region_6.8 | all-reduce | flops 4 | bytes 32 | tf_op jit(solution)/shard_map/psum | solution.py:126
  127.0 18.5 %psum.45 = f32[4]{0:T(128)S(1)} all-reduce(f32[4]{0:T(128)S(1)} %add.218), channel_id=1, replica_groups=mesh['grp'=2,'ew'=4,'ns'=2,'lvl'=2] {'ew','ns'}, use_global_device_ids=true, to_apply=%region_9.11 | all-reduce | flops 4 | bytes 32 | tf_op jit(solution)/shard_map/psum | solution.py:77
  145.8 1.3 collective-permute-start.27
  147.1 4.5 %collective-permute-start.26 = (f32[4,1,128]{2,1,0:T(1,128)S(1)}, f32[4,1,128]{2,1,0:T(1,128)S(1)}, u32[]{:S(2)}, u32[]{:S(2)}) collective-permute-start(f32[4,1,128]{2,1,0:T(1,128)S(1)} %get-tuple-element.158), channel_id=1, source_target_pairs={{0,4},{4,8},{8,12},{1,5},{5,9},{9,13},{2,6},{6,10},{10,14},{3,7},{... | collective-permute-start | bytes 6152 | tf_op jit(solution)/shard_map/ppermute | solution.py:14
  153.0 2.5 %collective-permute-start.31 = (f32[4,18,1]{2,1,0:T(8,128)S(1)}, f32[4,18,1]{2,1,0:T(8,128)S(1)}, u32[]{:S(2)}, u32[]{:S(2)}) collective-permute-start(f32[4,18,1]{2,1,0:T(8,128)S(1)} %get-tuple-element.149), channel_id=1, source_target_pairs={{0,2},{1,3},{4,6},{5,7},{8,10},{9,11},{12,14},{13,15},{16,18},{17,... | collective-permute-start | bytes 872 | tf_op jit(solution)/shard_map/ppermute | solution.py:14
  155.5 1.3 collective-permute-start.30
  156.8 1.3 collective-permute-start.18
  158.1 4.8 %collective-permute-start.19 = (f32[4,1,256]{2,0,1:T(4,128)S(1)}, f32[4,1,256]{2,0,1:T(4,128)S(1)}, u32[]{:S(2)}, u32[]{:S(2)}) collective-permute-start(f32[4,1,256]{2,0,1:T(4,128)S(1)} %get-tuple-element.140), channel_id=1, source_target_pairs={{0,4},{4,8},{8,12},{1,5},{5,9},{9,13},{2,6},{6,10},{10,14},{3,7},{... | collective-permute-start | bytes 12296 | tf_op jit(solution)/shard_map/ppermute | solution.py:14
  163.1 1.3 collective-permute-start.32
  164.4 4.6 %collective-permute-start.33 = (f32[4,1,128]{2,1,0:T(1,128)S(1)}, f32[4,1,128]{2,1,0:T(1,128)S(1)}, u32[]{:S(2)}, u32[]{:S(2)}) collective-permute-start(f32[4,1,128]{2,1,0:T(1,128)S(1)} %get-tuple-element.156), channel_id=1, source_target_pairs={{0,4},{4,8},{8,12},{1,5},{5,9},{9,13},{2,6},{6,10},{10,14},{3,7},{... | collective-permute-start | bytes 6152 | tf_op jit(solution)/shard_map/ppermute | solution.py:14
  169.8 15.5 %fusion = f32[4,128,128]{2,0,1:T(4,128)S(1)} fusion(f32[128,128,128]{2,1,0:T(8,128)} %param.30, f32[128,4,128]{2,1,0:T(4,128)S(1)} %gather_fusion.1, f32[128,128]{1,0:T(8,128)S(1)} %broadcast_multiply_fusion, pred[128]{0:T(512)(128)(4,1)S(1)} %compare_and_fusion), kind=kOutput, calls=%fused_computation.3 | convolution fusion | flops 100794368 | bytes 8978560 | tf_op jit(solution)/shard_map/bij,pbj->pbi/dot_general | solution.py:92
  185.3 9.4 %fusion.93 = f32[128,4,128]{2,1,0:T(4,128)S(1)} fusion(f32[4,128,128]{2,0,1:T(4,128)S(1)} %fusion, f32[128,128,128]{2,1,0:T(8,128)} %param.30), kind=kOutput, calls=%fused_computation.210 | convolution fusion | flops 100663296 | bytes 8912896 | tf_op jit(solution)/shard_map/bij,pbi->pbj/dot_general | solution.py:100
  195.2 3.9 %collective-permute-start.28 = (f32[4,384]{1,0:T(4,128)S(1)}, f32[4,384]{1,0:T(4,128)S(1)}, u32[]{:S(2)}, u32[]{:S(2)}) collective-permute-start(f32[4,384]{1,0:T(4,128)S(1)} %pad_maximum_fusion.76), channel_id=1, source_target_pairs={{0,4},{4,8},{8,12},{1,5},{5,9},{9,13},{2,6},{6,10},{10,14},{3,7},{... | collective-permute-start | bytes 18440 | tf_op jit(solution)/shard_map/ppermute | solution.py:25
  199.1 4.6 %collective-permute-start.21 = (f32[4,34,1]{2,0,1:T(4,128)S(1)}, f32[4,34,1]{2,0,1:T(4,128)S(1)}, u32[]{:S(2)}, u32[]{:S(2)}) collective-permute-start(f32[4,34,1]{2,0,1:T(4,128)S(1)} %get-tuple-element.129), channel_id=1, source_target_pairs={{0,2},{1,3},{4,6},{5,7},{8,10},{9,11},{12,14},{13,15},{16,18},{17,... | collective-permute-start | bytes 1640 | tf_op jit(solution)/shard_map/ppermute | solution.py:14
  203.7 1.3 collective-permute-start.20
  205.6 4.3 %collective-permute-done.20 = f32[4,34,1]{2,0,1:T(4,128)S(1)} collective-permute-done((f32[4,34,1]{2,0,1:T(4,128)S(1)}, f32[4,34,1]{2,0,1:T(4,128)S(1)}, u32[]{:S(2)}, u32[]{:S(2)}) %collective-permute-start.20) | collective-permute-done | bytes 576 | tf_op jit(solution)/shard_map/ppermute | solution.py:17
  210.1 1.3 collective-permute-start.22
  211.4 4.5 %collective-permute-start.23 = (f32[4,1,256]{2,0,1:T(4,128)S(1)}, f32[4,1,256]{2,0,1:T(4,128)S(1)}, u32[]{:S(2)}, u32[]{:S(2)}) collective-permute-start(f32[4,1,256]{2,0,1:T(4,128)S(1)} %get-tuple-element.138), channel_id=1, source_target_pairs={{0,4},{4,8},{8,12},{1,5},{5,9},{9,13},{2,6},{6,10},{10,14},{3,7},{... | collective-permute-start | bytes 12296 | tf_op jit(solution)/shard_map/ppermute | solution.py:14
  216.1 1.6 collective-permute-start.35
  219.1 4.5 %collective-permute-start.25 = (f32[4,34,1]{2,0,1:T(4,128)S(1)}, f32[4,34,1]{2,0,1:T(4,128)S(1)}, u32[]{:S(2)}, u32[]{:S(2)}) collective-permute-start(f32[4,34,1]{2,0,1:T(4,128)S(1)} %get-tuple-element.127), channel_id=1, source_target_pairs={{0,2},{1,3},{4,6},{5,7},{8,10},{9,11},{12,14},{13,15},{16,18},{17,... | collective-permute-start | bytes 1640 | tf_op jit(solution)/shard_map/ppermute | solution.py:14
  226.3 4.2 %collective-permute-done.29 = f32[4,384]{1,0:T(4,128)S(1)} collective-permute-done((f32[4,384]{1,0:T(4,128)S(1)}, f32[4,384]{1,0:T(4,128)S(1)}, u32[]{:S(2)}, u32[]{:S(2)}) %collective-permute-start.29) | collective-permute-done | bytes 6176 | tf_op jit(solution)/shard_map/ppermute | solution.py:25
  231.2 5.5 %psum.46 = f32[4]{0:T(128)S(1)} all-reduce(f32[4]{0:T(128)S(1)} %add.239), channel_id=1, replica_groups=mesh['grp'=2,'ew'=4,'ns'=2,'lvl'=2] {'ns'}, use_global_device_ids=true, to_apply=%region_12.14 | all-reduce | flops 4 | bytes 32 | tf_op jit(solution)/shard_map/psum | solution.py:126
  236.7 8.4 %psum.47 = f32[4]{0:T(128)S(1)} all-reduce(f32[4]{0:T(128)S(1)} %psum.46), channel_id=1, replica_groups=mesh['grp'=2,'ew'=4,'ns'=2,'lvl'=2] {'ew'}, use_global_device_ids=true, to_apply=%region_13.15 | all-reduce | flops 4 | bytes 32 | tf_op jit(solution)/shard_map/psum | solution.py:126
  (141 shorter events, 20.4 us)
Async XLA Ops:
  1.4 18.1 %collective-permute-start.9 = (f32[4,1,128]{2,1,0:T(1,128)S(1)}, f32[4,1,128]{2,1,0:T(1,128)S(1)}, u32[]{:S(2)}, u32[]{:S(2)}) collective-permute-start(f32[4,1,128]{2,1,0:T(1,128)S(1)} %get-tuple-element.163), channel_id=1, source_target_pairs={{4,0},{8,4},{12,8},{5,1},{9,5},{13,9},{6,2},{10,6},{14,10},{7,3},{... | collective-permute-start | bytes 6152 | tf_op jit(solution)/shard_map/ppermute | solution.py:17
  2.7 16.8 %collective-permute-start.8 = (f32[4,1,128]{2,1,0:T(1,128)S(1)}, f32[4,1,128]{2,1,0:T(1,128)S(1)}, u32[]{:S(2)}, u32[]{:S(2)}) collective-permute-start(f32[4,1,128]{2,1,0:T(1,128)S(1)} %get-tuple-element.162), channel_id=1, source_target_pairs={{0,4},{4,8},{8,12},{1,5},{5,9},{9,13},{2,6},{6,10},{10,14},{3,7},{... | collective-permute-start | bytes 6152 | tf_op jit(solution)/shard_map/ppermute | solution.py:14
  9.3 26.1 %collective-permute-start = (f32[4,1,256]{2,0,1:T(4,128)S(1)}, f32[4,1,256]{2,0,1:T(4,128)S(1)}, u32[]{:S(2)}, u32[]{:S(2)}) collective-permute-start(f32[4,1,256]{2,0,1:T(4,128)S(1)} %get-tuple-element.145), channel_id=1, source_target_pairs={{4,0},{8,4},{12,8},{5,1},{9,5},{13,9},{6,2},{10,6},{14,10},{7,3},{... | collective-permute-start | bytes 12296 | tf_op jit(solution)/shard_map/ppermute | solution.py:17
  10.6 24.8 %collective-permute-start.1 = (f32[4,1,256]{2,0,1:T(4,128)S(1)}, f32[4,1,256]{2,0,1:T(4,128)S(1)}, u32[]{:S(2)}, u32[]{:S(2)}) collective-permute-start(f32[4,1,256]{2,0,1:T(4,128)S(1)} %get-tuple-element.144), channel_id=1, source_target_pairs={{0,4},{4,8},{8,12},{1,5},{5,9},{9,13},{2,6},{6,10},{10,14},{3,7},{... | collective-permute-start | bytes 12296 | tf_op jit(solution)/shard_map/ppermute | solution.py:14
  19.6 5.6 %collective-permute-start.13 = (f32[4,18,1]{2,1,0:T(8,128)S(1)}, f32[4,18,1]{2,1,0:T(8,128)S(1)}, u32[]{:S(2)}, u32[]{:S(2)}) collective-permute-start(f32[4,18,1]{2,1,0:T(8,128)S(1)} %get-tuple-element.153), channel_id=1, source_target_pairs={{0,2},{1,3},{4,6},{5,7},{8,10},{9,11},{12,14},{13,15},{16,18},{17,... | collective-permute-start | bytes 872 | tf_op jit(solution)/shard_map/ppermute | solution.py:14
  23.5 6.0 %collective-permute-start.12 = (f32[4,18,1]{2,1,0:T(8,128)S(1)}, f32[4,18,1]{2,1,0:T(8,128)S(1)}, u32[]{:S(2)}, u32[]{:S(2)}) collective-permute-start(f32[4,18,1]{2,1,0:T(8,128)S(1)} %get-tuple-element.152), channel_id=1, source_target_pairs={{2,0},{3,1},{6,4},{7,5},{10,8},{11,9},{14,12},{15,13},{18,16},{19,... | collective-permute-start | bytes 872 | tf_op jit(solution)/shard_map/ppermute | solution.py:17
  29.6 37.6 %collective-permute-start.14 = (f32[4,1,128]{2,1,0:T(1,128)S(1)}, f32[4,1,128]{2,1,0:T(1,128)S(1)}, u32[]{:S(2)}, u32[]{:S(2)}) collective-permute-start(f32[4,1,128]{2,1,0:T(1,128)S(1)} %get-tuple-element.161), channel_id=1, source_target_pairs={{4,0},{8,4},{12,8},{5,1},{9,5},{13,9},{6,2},{10,6},{14,10},{7,3},{... | collective-permute-start | bytes 6152 | tf_op jit(solution)/shard_map/ppermute | solution.py:17
  30.9 36.4 %collective-permute-start.15 = (f32[4,1,128]{2,1,0:T(1,128)S(1)}, f32[4,1,128]{2,1,0:T(1,128)S(1)}, u32[]{:S(2)}, u32[]{:S(2)}) collective-permute-start(f32[4,1,128]{2,1,0:T(1,128)S(1)} %get-tuple-element.160), channel_id=1, source_target_pairs={{0,4},{4,8},{8,12},{1,5},{5,9},{9,13},{2,6},{6,10},{10,14},{3,7},{... | collective-permute-start | bytes 6152 | tf_op jit(solution)/shard_map/ppermute | solution.py:14
  36.3 16.4 %copy-start = (f32[128,128,128]{2,1,0:T(8,128)S(1)}, f32[128,128,128]{2,1,0:T(8,128)}, u32[]{:S(2)}) copy-start(f32[128,128,128]{2,1,0:T(8,128)} %param.30) | copy-start | bytes 25165828
  36.3 23.7 %copy-start.3 = (s32[128]{0:T(128)S(1)}, s32[128]{0:T(128)}, u32[]{:S(2)}) copy-start(s32[128]{0:T(128)} %param.32) | copy-start | bytes 1540
  36.3 56.5 %copy-start.1 = (s32[4,32,256]{2,1,0:T(8,128)S(1)}, s32[4,32,256]{2,1,0:T(8,128)}, u32[]{:S(2)}) copy-start(s32[4,32,256]{2,1,0:T(8,128)} %param.26) | copy-start | bytes 393220
  52.7 40.5 %copy-start.2 = (s32[4,16,128]{2,1,0:T(8,128)S(1)}, s32[4,16,128]{2,1,0:T(8,128)}, u32[]{:S(2)}) copy-start(s32[4,16,128]{2,1,0:T(8,128)} %param.27) | copy-start | bytes 98308
  60.6 26.6 %collective-permute-start.10 = (f32[4,384]{1,0:T(4,128)S(1)}, f32[4,384]{1,0:T(4,128)S(1)}, u32[]{:S(2)}, u32[]{:S(2)}) collective-permute-start(f32[4,384]{1,0:T(4,128)S(1)} %pad_maximum_fusion.74), channel_id=1, source_target_pairs={{0,4},{4,8},{8,12},{1,5},{5,9},{9,13},{2,6},{6,10},{10,14},{3,7},{... | collective-permute-start | bytes 18440 | tf_op jit(solution)/shard_map/ppermute | solution.py:25
  64.1 3.5 %collective-permute-start.3 = (f32[4,34,1]{2,0,1:T(4,128)S(1)}, f32[4,34,1]{2,0,1:T(4,128)S(1)}, u32[]{:S(2)}, u32[]{:S(2)}) collective-permute-start(f32[4,34,1]{2,0,1:T(4,128)S(1)} %get-tuple-element.135), channel_id=1, source_target_pairs={{0,2},{1,3},{4,6},{5,7},{8,10},{9,11},{12,14},{13,15},{16,18},{17,... | collective-permute-start | bytes 1640 | tf_op jit(solution)/shard_map/ppermute | solution.py:14
  65.7 6.4 %collective-permute-start.2 = (f32[4,34,1]{2,0,1:T(4,128)S(1)}, f32[4,34,1]{2,0,1:T(4,128)S(1)}, u32[]{:S(2)}, u32[]{:S(2)}) collective-permute-start(f32[4,34,1]{2,0,1:T(4,128)S(1)} %get-tuple-element.134), channel_id=1, source_target_pairs={{2,0},{3,1},{6,4},{7,5},{10,8},{11,9},{14,12},{15,13},{18,16},{19,... | collective-permute-start | bytes 1640 | tf_op jit(solution)/shard_map/ppermute | solution.py:17
  72.4 8.8 %collective-permute-start.4 = (f32[4,1,256]{2,0,1:T(4,128)S(1)}, f32[4,1,256]{2,0,1:T(4,128)S(1)}, u32[]{:S(2)}, u32[]{:S(2)}) collective-permute-start(f32[4,1,256]{2,0,1:T(4,128)S(1)} %get-tuple-element.143), channel_id=1, source_target_pairs={{4,0},{8,4},{12,8},{5,1},{9,5},{13,9},{6,2},{10,6},{14,10},{7,3},{... | collective-permute-start | bytes 12296 | tf_op jit(solution)/shard_map/ppermute | solution.py:17
  73.7 7.5 %collective-permute-start.5 = (f32[4,1,256]{2,0,1:T(4,128)S(1)}, f32[4,1,256]{2,0,1:T(4,128)S(1)}, u32[]{:S(2)}, u32[]{:S(2)}) collective-permute-start(f32[4,1,256]{2,0,1:T(4,128)S(1)} %get-tuple-element.142), channel_id=1, source_target_pairs={{0,4},{4,8},{8,12},{1,5},{5,9},{9,13},{2,6},{6,10},{10,14},{3,7},{... | collective-permute-start | bytes 12296 | tf_op jit(solution)/shard_map/ppermute | solution.py:14
  78.3 14.9 %collective-permute-start.17 = (f32[4,18,1]{2,1,0:T(8,128)S(1)}, f32[4,18,1]{2,1,0:T(8,128)S(1)}, u32[]{:S(2)}, u32[]{:S(2)}) collective-permute-start(f32[4,18,1]{2,1,0:T(8,128)S(1)} %get-tuple-element.151), channel_id=1, source_target_pairs={{0,2},{1,3},{4,6},{5,7},{8,10},{9,11},{12,14},{13,15},{16,18},{17,... | collective-permute-start | bytes 872 | tf_op jit(solution)/shard_map/ppermute | solution.py:14
  79.9 13.4 %collective-permute-start.16 = (f32[4,18,1]{2,1,0:T(8,128)S(1)}, f32[4,18,1]{2,1,0:T(8,128)S(1)}, u32[]{:S(2)}, u32[]{:S(2)}) collective-permute-start(f32[4,18,1]{2,1,0:T(8,128)S(1)} %get-tuple-element.150), channel_id=1, source_target_pairs={{2,0},{3,1},{6,4},{7,5},{10,8},{11,9},{14,12},{15,13},{18,16},{19,... | collective-permute-start | bytes 872 | tf_op jit(solution)/shard_map/ppermute | solution.py:17
  81.3 11.4 %collective-permute-start.7 = (f32[4,34,1]{2,0,1:T(4,128)S(1)}, f32[4,34,1]{2,0,1:T(4,128)S(1)}, u32[]{:S(2)}, u32[]{:S(2)}) collective-permute-start(f32[4,34,1]{2,0,1:T(4,128)S(1)} %get-tuple-element.133), channel_id=1, source_target_pairs={{0,2},{1,3},{4,6},{5,7},{8,10},{9,11},{12,14},{13,15},{16,18},{17,... | collective-permute-start | bytes 1640 | tf_op jit(solution)/shard_map/ppermute | solution.py:14
  85.9 6.9 %collective-permute-start.6 = (f32[4,34,1]{2,0,1:T(4,128)S(1)}, f32[4,34,1]{2,0,1:T(4,128)S(1)}, u32[]{:S(2)}, u32[]{:S(2)}) collective-permute-start(f32[4,34,1]{2,0,1:T(4,128)S(1)} %get-tuple-element.132), channel_id=1, source_target_pairs={{2,0},{3,1},{6,4},{7,5},{10,8},{11,9},{14,12},{15,13},{18,16},{19,... | collective-permute-start | bytes 1640 | tf_op jit(solution)/shard_map/ppermute | solution.py:17
  87.2 5.5 %collective-permute-start.11 = (f32[4,384]{1,0:T(4,128)S(1)}, f32[4,384]{1,0:T(4,128)S(1)}, u32[]{:S(2)}, u32[]{:S(2)}) collective-permute-start(f32[4,384]{1,0:T(4,128)S(1)} %pad_maximum_fusion.75), channel_id=1, source_target_pairs={{4,0},{8,4},{12,8},{5,1},{9,5},{13,9},{6,2},{10,6},{14,10},{7,3},{... | collective-permute-start | bytes 18440 | tf_op jit(solution)/shard_map/ppermute | solution.py:25
  145.8 5.9 %collective-permute-start.27 = (f32[4,1,128]{2,1,0:T(1,128)S(1)}, f32[4,1,128]{2,1,0:T(1,128)S(1)}, u32[]{:S(2)}, u32[]{:S(2)}) collective-permute-start(f32[4,1,128]{2,1,0:T(1,128)S(1)} %get-tuple-element.159), channel_id=1, source_target_pairs={{4,0},{8,4},{12,8},{5,1},{9,5},{13,9},{6,2},{10,6},{14,10},{7,3},{... | collective-permute-start | bytes 6152 | tf_op jit(solution)/shard_map/ppermute | solution.py:17
  147.1 5.8 %collective-permute-start.26 = (f32[4,1,128]{2,1,0:T(1,128)S(1)}, f32[4,1,128]{2,1,0:T(1,128)S(1)}, u32[]{:S(2)}, u32[]{:S(2)}) collective-permute-start(f32[4,1,128]{2,1,0:T(1,128)S(1)} %get-tuple-element.158), channel_id=1, source_target_pairs={{0,4},{4,8},{8,12},{1,5},{5,9},{9,13},{2,6},{6,10},{10,14},{3,7},{... | collective-permute-start | bytes 6152 | tf_op jit(solution)/shard_map/ppermute | solution.py:14
  153.0 9.9 %collective-permute-start.31 = (f32[4,18,1]{2,1,0:T(8,128)S(1)}, f32[4,18,1]{2,1,0:T(8,128)S(1)}, u32[]{:S(2)}, u32[]{:S(2)}) collective-permute-start(f32[4,18,1]{2,1,0:T(8,128)S(1)} %get-tuple-element.149), channel_id=1, source_target_pairs={{0,2},{1,3},{4,6},{5,7},{8,10},{9,11},{12,14},{13,15},{16,18},{17,... | collective-permute-start | bytes 872 | tf_op jit(solution)/shard_map/ppermute | solution.py:14
  155.5 7.4 %collective-permute-start.30 = (f32[4,18,1]{2,1,0:T(8,128)S(1)}, f32[4,18,1]{2,1,0:T(8,128)S(1)}, u32[]{:S(2)}, u32[]{:S(2)}) collective-permute-start(f32[4,18,1]{2,1,0:T(8,128)S(1)} %get-tuple-element.148), channel_id=1, source_target_pairs={{2,0},{3,1},{6,4},{7,5},{10,8},{11,9},{14,12},{15,13},{18,16},{19,... | collective-permute-start | bytes 872 | tf_op jit(solution)/shard_map/ppermute | solution.py:17
  156.8 12.1 %collective-permute-start.18 = (f32[4,1,256]{2,0,1:T(4,128)S(1)}, f32[4,1,256]{2,0,1:T(4,128)S(1)}, u32[]{:S(2)}, u32[]{:S(2)}) collective-permute-start(f32[4,1,256]{2,0,1:T(4,128)S(1)} %get-tuple-element.141), channel_id=1, source_target_pairs={{4,0},{8,4},{12,8},{5,1},{9,5},{13,9},{6,2},{10,6},{14,10},{7,3},{... | collective-permute-start | bytes 12296 | tf_op jit(solution)/shard_map/ppermute | solution.py:17
  158.1 10.8 %collective-permute-start.19 = (f32[4,1,256]{2,0,1:T(4,128)S(1)}, f32[4,1,256]{2,0,1:T(4,128)S(1)}, u32[]{:S(2)}, u32[]{:S(2)}) collective-permute-start(f32[4,1,256]{2,0,1:T(4,128)S(1)} %get-tuple-element.140), channel_id=1, source_target_pairs={{0,4},{4,8},{8,12},{1,5},{5,9},{9,13},{2,6},{6,10},{10,14},{3,7},{... | collective-permute-start | bytes 12296 | tf_op jit(solution)/shard_map/ppermute | solution.py:14
  163.1 41.9 %collective-permute-start.32 = (f32[4,1,128]{2,1,0:T(1,128)S(1)}, f32[4,1,128]{2,1,0:T(1,128)S(1)}, u32[]{:S(2)}, u32[]{:S(2)}) collective-permute-start(f32[4,1,128]{2,1,0:T(1,128)S(1)} %get-tuple-element.157), channel_id=1, source_target_pairs={{4,0},{8,4},{12,8},{5,1},{9,5},{13,9},{6,2},{10,6},{14,10},{7,3},{... | collective-permute-start | bytes 6152 | tf_op jit(solution)/shard_map/ppermute | solution.py:17
  164.4 40.6 %collective-permute-start.33 = (f32[4,1,128]{2,1,0:T(1,128)S(1)}, f32[4,1,128]{2,1,0:T(1,128)S(1)}, u32[]{:S(2)}, u32[]{:S(2)}) collective-permute-start(f32[4,1,128]{2,1,0:T(1,128)S(1)} %get-tuple-element.156), channel_id=1, source_target_pairs={{0,4},{4,8},{8,12},{1,5},{5,9},{9,13},{2,6},{6,10},{10,14},{3,7},{... | collective-permute-start | bytes 6152 | tf_op jit(solution)/shard_map/ppermute | solution.py:14
  195.2 29.8 %collective-permute-start.28 = (f32[4,384]{1,0:T(4,128)S(1)}, f32[4,384]{1,0:T(4,128)S(1)}, u32[]{:S(2)}, u32[]{:S(2)}) collective-permute-start(f32[4,384]{1,0:T(4,128)S(1)} %pad_maximum_fusion.76), channel_id=1, source_target_pairs={{0,4},{4,8},{8,12},{1,5},{5,9},{9,13},{2,6},{6,10},{10,14},{3,7},{... | collective-permute-start | bytes 18440 | tf_op jit(solution)/shard_map/ppermute | solution.py:25
  199.1 6.5 %collective-permute-start.21 = (f32[4,34,1]{2,0,1:T(4,128)S(1)}, f32[4,34,1]{2,0,1:T(4,128)S(1)}, u32[]{:S(2)}, u32[]{:S(2)}) collective-permute-start(f32[4,34,1]{2,0,1:T(4,128)S(1)} %get-tuple-element.129), channel_id=1, source_target_pairs={{0,2},{1,3},{4,6},{5,7},{8,10},{9,11},{12,14},{13,15},{16,18},{17,... | collective-permute-start | bytes 1640 | tf_op jit(solution)/shard_map/ppermute | solution.py:14
  203.7 6.2 %collective-permute-start.20 = (f32[4,34,1]{2,0,1:T(4,128)S(1)}, f32[4,34,1]{2,0,1:T(4,128)S(1)}, u32[]{:S(2)}, u32[]{:S(2)}) collective-permute-start(f32[4,34,1]{2,0,1:T(4,128)S(1)} %get-tuple-element.128), channel_id=1, source_target_pairs={{2,0},{3,1},{6,4},{7,5},{10,8},{11,9},{14,12},{15,13},{18,16},{19,... | collective-permute-start | bytes 1640 | tf_op jit(solution)/shard_map/ppermute | solution.py:17
  210.1 8.8 %collective-permute-start.22 = (f32[4,1,256]{2,0,1:T(4,128)S(1)}, f32[4,1,256]{2,0,1:T(4,128)S(1)}, u32[]{:S(2)}, u32[]{:S(2)}) collective-permute-start(f32[4,1,256]{2,0,1:T(4,128)S(1)} %get-tuple-element.139), channel_id=1, source_target_pairs={{4,0},{8,4},{12,8},{5,1},{9,5},{13,9},{6,2},{10,6},{14,10},{7,3},{... | collective-permute-start | bytes 12296 | tf_op jit(solution)/shard_map/ppermute | solution.py:17
  211.4 7.5 %collective-permute-start.23 = (f32[4,1,256]{2,0,1:T(4,128)S(1)}, f32[4,1,256]{2,0,1:T(4,128)S(1)}, u32[]{:S(2)}, u32[]{:S(2)}) collective-permute-start(f32[4,1,256]{2,0,1:T(4,128)S(1)} %get-tuple-element.138), channel_id=1, source_target_pairs={{0,4},{4,8},{8,12},{1,5},{5,9},{9,13},{2,6},{6,10},{10,14},{3,7},{... | collective-permute-start | bytes 12296 | tf_op jit(solution)/shard_map/ppermute | solution.py:14
  216.1 14.9 %collective-permute-start.35 = (f32[4,18,1]{2,1,0:T(8,128)S(1)}, f32[4,18,1]{2,1,0:T(8,128)S(1)}, u32[]{:S(2)}, u32[]{:S(2)}) collective-permute-start(f32[4,18,1]{2,1,0:T(8,128)S(1)} %get-tuple-element.147), channel_id=1, source_target_pairs={{0,2},{1,3},{4,6},{5,7},{8,10},{9,11},{12,14},{13,15},{16,18},{17,... | collective-permute-start | bytes 872 | tf_op jit(solution)/shard_map/ppermute | solution.py:14
  217.6 13.3 %collective-permute-start.34 = (f32[4,18,1]{2,1,0:T(8,128)S(1)}, f32[4,18,1]{2,1,0:T(8,128)S(1)}, u32[]{:S(2)}, u32[]{:S(2)}) collective-permute-start(f32[4,18,1]{2,1,0:T(8,128)S(1)} %get-tuple-element.146), channel_id=1, source_target_pairs={{2,0},{3,1},{6,4},{7,5},{10,8},{11,9},{14,12},{15,13},{18,16},{19,... | collective-permute-start | bytes 872 | tf_op jit(solution)/shard_map/ppermute | solution.py:17
  219.1 11.4 %collective-permute-start.25 = (f32[4,34,1]{2,0,1:T(4,128)S(1)}, f32[4,34,1]{2,0,1:T(4,128)S(1)}, u32[]{:S(2)}, u32[]{:S(2)}) collective-permute-start(f32[4,34,1]{2,0,1:T(4,128)S(1)} %get-tuple-element.127), channel_id=1, source_target_pairs={{0,2},{1,3},{4,6},{5,7},{8,10},{9,11},{12,14},{13,15},{16,18},{17,... | collective-permute-start | bytes 1640 | tf_op jit(solution)/shard_map/ppermute | solution.py:14
  223.6 6.9 %collective-permute-start.24 = (f32[4,34,1]{2,0,1:T(4,128)S(1)}, f32[4,34,1]{2,0,1:T(4,128)S(1)}, u32[]{:S(2)}, u32[]{:S(2)}) collective-permute-start(f32[4,34,1]{2,0,1:T(4,128)S(1)} %get-tuple-element.126), channel_id=1, source_target_pairs={{2,0},{3,1},{6,4},{7,5},{10,8},{11,9},{14,12},{15,13},{18,16},{19,... | collective-permute-start | bytes 1640 | tf_op jit(solution)/shard_map/ppermute | solution.py:17
  225.0 5.5 %collective-permute-start.29 = (f32[4,384]{1,0:T(4,128)S(1)}, f32[4,384]{1,0:T(4,128)S(1)}, u32[]{:S(2)}, u32[]{:S(2)}) collective-permute-start(f32[4,384]{1,0:T(4,128)S(1)} %pad_maximum_fusion.77), channel_id=1, source_target_pairs={{4,0},{8,4},{12,8},{5,1},{9,5},{13,9},{6,2},{10,6},{14,10},{7,3},{... | collective-permute-start | bytes 18440 | tf_op jit(solution)/shard_map/ppermute | solution.py:25
